TPU v7x, 32 devices: a whole 2x2x4 slice. The times are simulated.
32 devices in a mesh: gx: 4 (over x, core), gy: 8 (over z, y).
Axes of the slice: x: 2, y: 2, z: 4, core: 2. Of those that a mesh axis runs over, the one named last changes fastest.
Arguments:
- forcing: float32 [8, 8, 8, 4, 8, 128], P(None, None, None, 'gx', 'gy'), may hold values from -6 to 6
- coefficient: float32 [8, 8, 8, 4, 8, 128], P(None, None, None, 'gx', 'gy'), may hold values from 0.3 to 3
Outputs:
- pressure: float32 [8, 8, 8, 4, 8, 128], P(None, None, None, 'gx', 'gy')
- residual: float32 [8, 8, 8, 4, 8, 128], P(None, None, None, 'gx', 'gy')
All inputs are finite; a program needn't handle non-finite values.
Results may differ from a plain program's by a relative error of at most 0.0003.
Values sent between devices are 32-bit elements; how exact they have to be, the bound alone decides.
A program may use at most 64 MiB of HBM per device.

v0:
```python
import math

import jax
import jax.numpy as jnp
from jax import lax
from jax.sharding import PartitionSpec as P

ITERS = 2


stretch = (1.0, 64.0, 1.0)


def with_halo(cells, sides, width):
    for axis, dim in sides:
        count = lax.axis_size(axis)
        ends = count - 1
        head = lax.slice_in_dim(cells, 0, width, axis=dim)
        tail = lax.slice_in_dim(cells, cells.shape[dim] - width, cells.shape[dim], axis=dim)
        cells = jnp.concatenate(
            [
                lax.ppermute(tail, axis, [(i, (i + 1) % count) for i in range(ends)]),
                cells,
                lax.ppermute(head, axis, [((i + 1) % count, i) for i in range(ends)]),
            ],
            axis=dim,
        )
    return cells


def legendre_value(order, position):
    prev_value = 1.0
    this_value = position
    for degree_now in range(2, order + 1):
        next_value = (
            (2 * degree_now - 1) * position * this_value - (degree_now - 1) * prev_value
        ) / degree_now
        prev_value = this_value
        this_value = next_value
    return this_value


def gll_points():
    points = [-1.0]
    for node_index in range(1, 7):
        position = -math.cos(math.pi * node_index / 7.0)
        for newton_step in range(60):
            target = legendre_value(8, position) - legendre_value(6, position)
            slope = 15.0 * legendre_value(7, position)
            position = position - target / slope
        points.append(position)
    points.append(1.0)
    return points


def jacobi_eigen(matrix_in):
    order_n = len(matrix_in)
    work_mat = [list(one_row) for one_row in matrix_in]
    vectors = [
        [1.0 if row_index == col_index else 0.0 for col_index in range(order_n)]
        for row_index in range(order_n)
    ]
    for sweep_index in range(40):
        for first_idx in range(order_n):
            for second_idx in range(first_idx + 1, order_n):
                rotation = 0.5 * math.atan2(
                    2.0 * work_mat[first_idx][second_idx],
                    work_mat[second_idx][second_idx] - work_mat[first_idx][first_idx],
                )
                cosine = math.cos(rotation)
                sine_part = math.sin(rotation)
                for other in range(order_n):
                    left_val = work_mat[other][first_idx]
                    right_val = work_mat[other][second_idx]
                    work_mat[other][first_idx] = cosine * left_val - sine_part * right_val
                    work_mat[other][second_idx] = sine_part * left_val + cosine * right_val
                for other in range(order_n):
                    left_val = work_mat[first_idx][other]
                    right_val = work_mat[second_idx][other]
                    work_mat[first_idx][other] = cosine * left_val - sine_part * right_val
                    work_mat[second_idx][other] = sine_part * left_val + cosine * right_val
                for other in range(order_n):
                    left_val = vectors[other][first_idx]
                    right_val = vectors[other][second_idx]
                    vectors[other][first_idx] = cosine * left_val - sine_part * right_val
                    vectors[other][second_idx] = sine_part * left_val + cosine * right_val
    return ([work_mat[diag_index][diag_index] for diag_index in range(order_n)], vectors)


def spectral_tables():
    nodes = gll_points()
    values_at = [legendre_value(7, position) for position in nodes]
    weights = [2.0 / (56.0 * value_now * value_now) for value_now in values_at]
    derivative = [[0.0] * 8 for row_index in range(8)]
    for row_index in range(8):
        for col_index in range(8):
            if row_index != col_index:
                derivative[row_index][col_index] = values_at[row_index] / (
                    values_at[col_index] * (nodes[row_index] - nodes[col_index])
                )
    derivative[0][0] = -14.0
    derivative[7][7] = 14.0
    stiffness = [
        [
            sum(
                (
                    derivative[mid][row_index] * weights[mid] * derivative[mid][col_index]
                    for mid in range(8)
                )
            )
            for col_index in range(8)
        ]
        for row_index in range(8)
    ]
    stiffness[0][0] = 2.0 * stiffness[0][0]
    stiffness[7][7] = 2.0 * stiffness[7][7]
    inv_root = [1.0 / math.sqrt(weight_now) for weight_now in weights]
    symmetric = [
        [
            inv_root[row_index] * stiffness[row_index][col_index] * inv_root[col_index]
            for col_index in range(8)
        ]
        for row_index in range(8)
    ]
    eigen_values, eigen_vectors = jacobi_eigen(symmetric)
    fdm_basis = [
        [inv_root[row_index] * eigen_vectors[row_index][col_index] for col_index in range(8)]
        for row_index in range(8)
    ]
    linear_hat = [
        [(1.0 - position) / 2.0 for position in nodes],
        [(1.0 + position) / 2.0 for position in nodes],
    ]
    return tuple(
        (
            jnp.asarray(one_table, dtype=jnp.float32)
            for one_table in (weights, derivative, fdm_basis, eigen_values, linear_hat)
        )
    )


def contract(form, table, field):
    return jnp.einsum(form, table, field, precision=lax.Precision.HIGHEST)


def edge_factors(local_count, offset, total_count):
    node_ids = jnp.arange(8, dtype=jnp.int32)[:, None]
    element_ids = offset + jnp.arange(local_count, dtype=jnp.int32)[None, :]
    at_first = node_ids == 0
    at_last = node_ids == 7
    outside = at_first & (element_ids == 0) | at_last & (element_ids == total_count - 1)
    shared = at_first & (element_ids > 0) | at_last & (element_ids < total_count - 1)
    keep_factor = jnp.where(outside, 0.0, 1.0).astype(jnp.float32)
    share_factor = jnp.where(shared, 0.5, 1.0).astype(jnp.float32)
    return (keep_factor, share_factor)


def node_masks(counts, offsets, totals):
    keep_x, share_x = edge_factors(counts[0], offsets[0], totals[0])
    keep_y, share_y = edge_factors(counts[1], offsets[1], totals[1])
    keep_z, share_z = edge_factors(counts[2], offsets[2], totals[2])
    keep_mask = (
        keep_x[:, None, None, :, None, None],
        keep_y[None, :, None, None, :, None],
        keep_z[None, None, :, None, None, :],
    )
    inv_mult = (
        share_x[:, None, None, :, None, None],
        share_y[None, :, None, None, :, None],
        share_z[None, None, :, None, None, :],
    )
    return (keep_mask, inv_mult)


def apply_factors(field, factors):
    return field * factors[0] * factors[1] * factors[2]


def no_neighbours(first_rim, last_rim, elem_dim):
    return (jnp.zeros_like(last_rim), jnp.zeros_like(first_rim))


def x_neighbours(first_rim, last_rim, elem_dim):
    stacked = jnp.stack([first_rim, last_rim], axis=2)
    extended = with_halo(stacked, (("gx", 2),), 1)
    return (extended[:, :, 0], extended[:, :, 3])


def y_neighbours(first_rim, last_rim, elem_dim):
    stacked = jnp.stack([first_rim, last_rim], axis=3)
    extended = with_halo(stacked, (("gy", 3),), 1)
    return (extended[:, :, :, 0], extended[:, :, :, 3])


def pair_sum(field, node_dim, remote):
    elem_dim = node_dim + 2
    first = jnp.take(field, 0, axis=node_dim)
    last_face = jnp.take(field, 7, axis=node_dim)
    count = first.shape[elem_dim]
    first_rim = lax.index_in_dim(first, 0, elem_dim, keepdims=False)
    last_rim = lax.index_in_dim(last_face, count - 1, elem_dim, keepdims=False)
    prev_last, next_first = remote(first_rim, last_rim, elem_dim)
    next_all = jnp.concatenate(
        [lax.slice_in_dim(first, 1, count, axis=elem_dim), jnp.expand_dims(next_first, elem_dim)],
        axis=elem_dim,
    )
    prev_all = jnp.concatenate(
        [
            jnp.expand_dims(prev_last, elem_dim),
            lax.slice_in_dim(last_face, 0, count - 1, axis=elem_dim),
        ],
        axis=elem_dim,
    )
    new_first = first + prev_all
    new_last = last_face + next_all
    middle = lax.slice_in_dim(field, 1, 7, axis=node_dim)
    return jnp.concatenate(
        [jnp.expand_dims(new_first, node_dim), middle, jnp.expand_dims(new_last, node_dim)],
        axis=node_dim,
    )


def direct_sum(field):
    field = pair_sum(field, 0, x_neighbours)
    field = pair_sum(field, 1, y_neighbours)
    return pair_sum(field, 2, no_neighbours)


def stiffness_apply(field, coefficient, derivative, weight_cube):
    scaled = coefficient * weight_cube
    grad_i = contract("pi,ijkxyz->pjkxyz", derivative, field)
    grad_j = contract("qj,ijkxyz->iqkxyz", derivative, field)
    grad_k = contract("rk,ijkxyz->ijrxyz", derivative, field)
    result = contract("pi,pjkxyz->ijkxyz", derivative, stretch[0] * scaled * grad_i)
    result = result + contract("qj,iqkxyz->ijkxyz", derivative, stretch[1] * scaled * grad_j)
    return result + contract("rk,ijrxyz->ijkxyz", derivative, stretch[2] * scaled * grad_k)


def fdm_apply(field, fdm_basis, denominator):
    moved = contract("ip,ijkxyz->pjkxyz", fdm_basis, field)
    moved = contract("jq,pjkxyz->pqkxyz", fdm_basis, moved)
    moved = contract("kr,pqkxyz->pqrxyz", fdm_basis, moved)
    moved = moved * denominator
    moved = contract("ip,pqrxyz->iqrxyz", fdm_basis, moved)
    moved = contract("jq,iqrxyz->ijrxyz", fdm_basis, moved)
    return contract("kr,ijrxyz->ijkxyz", fdm_basis, moved)


def restrict_corners(weighted, linear_hat):
    corners = contract("ai,ijkxyz->ajkxyz", linear_hat, weighted)
    corners = contract("bj,ajkxyz->abkxyz", linear_hat, corners)
    return contract("ck,abkxyz->abcxyz", linear_hat, corners)


def vertex_sum(corners):
    total_grid = jnp.zeros(
        (corners.shape[3] + 1, corners.shape[4] + 1, corners.shape[5] + 1), jnp.float32
    )
    for side_x in range(2):
        for side_y in range(2):
            for side_z in range(2):
                total_grid = total_grid + jnp.pad(
                    corners[side_x, side_y, side_z],
                    ((side_x, 1 - side_x), (side_y, 1 - side_y), (side_z, 1 - side_z)),
                )
    return total_grid


def prolong(vertices, linear_hat):
    count_x = vertices.shape[0] - 1
    count_y = vertices.shape[1] - 1
    count_z = vertices.shape[2] - 1
    corner_vals = jnp.stack(
        [
            jnp.stack(
                [
                    jnp.stack(
                        [
                            vertices[
                                side_x : side_x + count_x,
                                side_y : side_y + count_y,
                                side_z : side_z + count_z,
                            ]
                            for side_z in range(2)
                        ]
                    )
                    for side_y in range(2)
                ]
            )
            for side_x in range(2)
        ]
    )
    nodal = contract("ck,abcxyz->abkxyz", linear_hat, corner_vals)
    nodal = contract("bj,abkxyz->ajkxyz", linear_hat, nodal)
    return contract("ai,ajkxyz->ijkxyz", linear_hat, nodal)


def sine_system(cells):
    wave_ints = jnp.arange(1, cells, dtype=jnp.int32)
    product_ids = wave_ints[:, None] * wave_ints[None, :] % (2 * cells)
    sine_table = math.sqrt(2.0 / cells) * jnp.sin(math.pi * product_ids.astype(jnp.float32) / cells)
    cosines = jnp.cos(math.pi * wave_ints.astype(jnp.float32) / cells)
    stiff_eig = (2.0 - 2.0 * cosines) / 2.0
    mass_eig = 2.0 * (4.0 + 2.0 * cosines) / 6.0
    return (sine_table, stiff_eig, mass_eig)


def coarse_solve(vertices):
    interior = vertices[1:-1, 1:-1, 1:-1]
    table_x, stiff_x, mass_x = sine_system(vertices.shape[0] - 1)
    table_y, stiff_y, mass_y = sine_system(vertices.shape[1] - 1)
    table_z, stiff_z, mass_z = sine_system(vertices.shape[2] - 1)
    moved = contract("mi,ijk->mjk", table_x, interior)
    moved = contract("nj,mjk->mnk", table_y, moved)
    moved = contract("ok,mnk->mno", table_z, moved)
    denominator = (
        stretch[0] * stiff_x[:, None, None] * mass_y[None, :, None] * mass_z[None, None, :]
    )
    denominator = (
        denominator
        + stretch[1] * mass_x[:, None, None] * stiff_y[None, :, None] * mass_z[None, None, :]
    )
    denominator = (
        denominator
        + stretch[2] * mass_x[:, None, None] * mass_y[None, :, None] * stiff_z[None, None, :]
    )
    moved = moved / denominator
    moved = contract("mi,mno->ino", table_x, moved)
    moved = contract("nj,ino->ijo", table_y, moved)
    moved = contract("ok,ijo->ijk", table_z, moved)
    return jnp.pad(moved, 1)


def on_device(forcing, coefficient):
    weights, derivative, fdm_basis, eigen_values, linear_hat = spectral_tables()
    local_x = forcing.shape[3]
    local_y = forcing.shape[4]
    depth_count = forcing.shape[5]
    size_x = lax.axis_size("gx")
    size_y = lax.axis_size("gy")
    start_x = lax.axis_index("gx") * local_x
    start_y = lax.axis_index("gy") * local_y
    total_x = local_x * size_x
    total_y = local_y * size_y
    keep_mask, inv_mult = node_masks(
        (local_x, local_y, depth_count), (start_x, start_y, 0), (total_x, total_y, depth_count)
    )
    weight_cube = (weights[:, None, None] * weights[None, :, None] * weights[None, None, :])[
        :, :, :, None, None, None
    ]
    eigen_sum = (
        stretch[0] * eigen_values[:, None, None]
        + stretch[1] * eigen_values[None, :, None]
        + stretch[2] * eigen_values[None, None, :]
    )
    denominator = (1.0 / eigen_sum)[:, :, :, None, None, None]

    def operate(field):
        return apply_factors(
            direct_sum(stiffness_apply(field, coefficient, derivative, weight_cube)), keep_mask
        )

    def coarse_part(field):
        vertices = vertex_sum(restrict_corners(apply_factors(field, inv_mult), linear_hat))
        whole_grid = jnp.zeros((total_x + 1, total_y + 1, depth_count + 1), jnp.float32)
        whole_grid = lax.dynamic_update_slice(
            whole_grid, vertices, (start_x, start_y, jnp.int32(0))
        )
        whole_grid = lax.psum(whole_grid, ("gx", "gy"))
        solved = coarse_solve(whole_grid)
        own_block = lax.dynamic_slice(solved, (start_x, start_y, jnp.int32(0)), vertices.shape)
        return prolong(own_block, linear_hat)

    def precondition(field):
        local_part = apply_factors(direct_sum(fdm_apply(field, fdm_basis, denominator)), keep_mask)
        return local_part + coarse_part(field)

    def inner_sum(left, right):
        return jnp.sum(apply_factors(left * right, inv_mult))

    def pair_total(left, middle_vec, right):
        return lax.psum((inner_sum(left, middle_vec), inner_sum(middle_vec, right)), ("gx", "gy"))

    load_vec = apply_factors(direct_sum(forcing), keep_mask)
    pressure = jnp.zeros_like(load_vec)
    residual = load_vec
    smoothed = precondition(residual)
    image_dir = operate(smoothed)
    energy_now, curve_now = pair_total(residual, smoothed, image_dir)
    step_size = energy_now / curve_now
    direction = smoothed
    along_dir = image_dir
    for step_index in range(ITERS):
        pressure = pressure + step_size * direction
        residual = residual - step_size * along_dir
        if step_index + 1 < ITERS:
            smoothed = precondition(residual)
            image_dir = operate(smoothed)
            energy_next, curve_now = pair_total(residual, smoothed, image_dir)
            ratio_now = energy_next / energy_now
            step_size = energy_next / (curve_now - ratio_now * energy_next / step_size)
            direction = smoothed + ratio_now * direction
            along_dir = image_dir + ratio_now * along_dir
            energy_now = energy_next
    return (pressure, residual)


def solution(mesh):
    in_specs = (P(None, None, None, "gx", "gy", None), P(None, None, None, "gx", "gy", None))
    out_specs = (P(None, None, None, "gx", "gy", None), P(None, None, None, "gx", "gy", None))
    return jax.shard_map(
        on_device, mesh=mesh, in_specs=in_specs, out_specs=out_specs, check_vma=False
    )
```

profile of v0, /device:TPU:0, one launch (start us, length us, event | category | flops | bytes accessed | tf_op | source)
XLA Modules:
  0.0 298.2 jit_solution(13644749835126306988)
XLA Ops:
  1.5 2.3 collective-permute-start
  3.9 1.3 collective-permute-start.1
  6.1 3.0 collective-permute-done.1
  9.1 3.4 %collective-permute-start.2 = (f32[8,8,1,1,128]{4,0,1,3,2:T(8,128)S(1)}, f32[8,8,1,1,128]{4,0,1,3,2:T(8,128)S(1)}, u32[]{:S(2)}, u32[]{:S(2)}) collective-permute-start(f32[8,8,1,1,128]{4,0,1,3,2:T(8,128)S(1)} %maximum_bitcast_fusion.16), channel_id=1, source_target_pairs={{0,1},{1,2},{2,3},{3,4},{4,5},{5,6},{6,7},{8,9},{9,10},{10,11},{11... | collective-permute-start | bytes 98312 | tf_op jit(solution)/shard_map/ppermute | solution.py:22
  12.6 1.6 collective-permute-done.2
  14.1 1.3 collective-permute-start.3
  15.6 4.6 %collective-permute-done.3 = f32[8,8,1,1,128]{4,0,1,3,2:T(8,128)S(1)} collective-permute-done((f32[8,8,1,1,128]{4,0,1,3,2:T(8,128)S(1)}, f32[8,8,1,1,128]{4,0,1,3,2:T(8,128)S(1)}, u32[]{:S(2)}, u32[]{:S(2)}) %collective-permute-start.3) | collective-permute-done | bytes 32800 | tf_op jit(solution)/shard_map/ppermute | solution.py:24
  22.4 43.6 %psum.42 = f32[5,9,129]{2,1,0:T(8,128)S(1)} all-reduce(f32[5,9,129]{2,1,0:T(8,128)S(1)} %dynamic_update_slice.6), channel_id=1, replica_groups=mesh['gx'=4,'gy'=8] {'gx','gy'}, use_global_device_ids=true, to_apply=%region_0.7 | all-reduce | flops 5805 | bytes 46440 | tf_op jit(solution)/shard_map/psum | solution.py:369
  72.9 1.3 collective-permute-start.5
  74.7 3.9 %collective-permute-done.5 = f32[8,8,1,1,128]{4,1,0,3,2:T(8,128)S(1)} collective-permute-done((f32[8,8,1,1,128]{4,1,0,3,2:T(8,128)S(1)}, f32[8,8,1,1,128]{4,1,0,3,2:T(8,128)S(1)}, u32[]{:S(2)}, u32[]{:S(2)}) %collective-permute-start.5) | collective-permute-done | bytes 32800 | tf_op jit(solution)/shard_map/ppermute | solution.py:24
  78.6 2.5 collective-permute-start.6
  81.4 1.3 collective-permute-done.6
  84.4 4.4 %collective-permute-done.7 = f32[8,8,1,1,128]{4,1,0,3,2:T(8,128)S(1)} collective-permute-done((f32[8,8,1,1,128]{4,1,0,3,2:T(8,128)S(1)}, f32[8,8,1,1,128]{4,1,0,3,2:T(8,128)S(1)}, u32[]{:S(2)}, u32[]{:S(2)}) %collective-permute-start.7) | collective-permute-done | bytes 32800 | tf_op jit(solution)/shard_map/ppermute | solution.py:24
  93.6 2.5 collective-permute-start.8
  97.6 3.2 %collective-permute-done.9 = f32[8,8,1,1,128]{4,1,0,3,2:T(8,128)S(1)} collective-permute-done((f32[8,8,1,1,128]{4,1,0,3,2:T(8,128)S(1)}, f32[8,8,1,1,128]{4,1,0,3,2:T(8,128)S(1)}, u32[]{:S(2)}, u32[]{:S(2)}) %collective-permute-start.9) | collective-permute-done | bytes 32800 | tf_op jit(solution)/shard_map/ppermute | solution.py:24
  100.8 4.8 %collective-permute-start.10 = (f32[8,8,1,1,128]{4,0,1,3,2:T(8,128)S(1)}, f32[8,8,1,1,128]{4,0,1,3,2:T(8,128)S(1)}, u32[]{:S(2)}, u32[]{:S(2)}) collective-permute-start(f32[8,8,1,1,128]{4,0,1,3,2:T(8,128)S(1)} %maximum_bitcast_fusion.10), channel_id=1, source_target_pairs={{0,1},{1,2},{2,3},{3,4},{4,5},{5,6},{6,7},{8,9},{9,10},{10,11},{11... | collective-permute-start | bytes 98312 | tf_op jit(solution)/shard_map/ppermute | solution.py:22
  107.2 1.5 collective-permute-start.11
  108.9 4.4 %collective-permute-done.11 = f32[8,8,1,1,128]{4,0,1,3,2:T(8,128)S(1)} collective-permute-done((f32[8,8,1,1,128]{4,0,1,3,2:T(8,128)S(1)}, f32[8,8,1,1,128]{4,0,1,3,2:T(8,128)S(1)}, u32[]{:S(2)}, u32[]{:S(2)}) %collective-permute-start.11) | collective-permute-done | bytes 32800 | tf_op jit(solution)/shard_map/ppermute | solution.py:24
  114.5 42.9 %all-reduce.29 = (f32[]{:T(128)}, f32[]{:T(128)}) all-reduce(f32[]{:T(128)} %fusion.76, f32[]{:T(128)} %multiply_reduce_fusion.1), channel_id=1, replica_groups=mesh['gx'=4,'gy'=8] {'gx','gy'}, use_global_device_ids=true, to_apply=%region_2.9 | all-reduce | flops 2 | bytes 16 | tf_op jit(solution)/shard_map/psum | solution.py:382
  160.1 40.8 %psum.45 = f32[5,9,129]{2,1,0:T(8,128)S(1)} all-reduce(f32[5,9,129]{2,1,0:T(8,128)S(1)} %dynamic_update_slice.7), channel_id=1, replica_groups=mesh['gx'=4,'gy'=8] {'gx','gy'}, use_global_device_ids=true, to_apply=%region_5.12 | all-reduce | flops 5805 | bytes 46440 | tf_op jit(solution)/shard_map/psum | solution.py:369
  207.9 1.3 collective-permute-start.13
  209.9 3.6 %collective-permute-done.13 = f32[8,8,1,1,128]{4,1,0,3,2:T(8,128)S(1)} collective-permute-done((f32[8,8,1,1,128]{4,1,0,3,2:T(8,128)S(1)}, f32[8,8,1,1,128]{4,1,0,3,2:T(8,128)S(1)}, u32[]{:S(2)}, u32[]{:S(2)}) %collective-permute-start.13) | collective-permute-done | bytes 32800 | tf_op jit(solution)/shard_map/ppermute | solution.py:24
  213.6 2.5 collective-permute-start.14
  217.7 1.3 collective-permute-start.15
  219.2 4.6 %collective-permute-done.15 = f32[8,8,1,1,128]{4,0,1,3,2:T(8,128)S(1)} collective-permute-done((f32[8,8,1,1,128]{4,0,1,3,2:T(8,128)S(1)}, f32[8,8,1,1,128]{4,0,1,3,2:T(8,128)S(1)}, u32[]{:S(2)}, u32[]{:S(2)}) %collective-permute-start.15) | collective-permute-done | bytes 32800 | tf_op jit(solution)/shard_map/ppermute | solution.py:24
  227.6 2.5 collective-permute-start.16
  230.2 1.5 collective-permute-start.17
  231.9 2.9 collective-permute-done.17
  234.8 4.8 %collective-permute-start.18 = (f32[8,8,1,1,128]{4,0,1,3,2:T(8,128)S(1)}, f32[8,8,1,1,128]{4,0,1,3,2:T(8,128)S(1)}, u32[]{:S(2)}, u32[]{:S(2)}) collective-permute-start(f32[8,8,1,1,128]{4,0,1,3,2:T(8,128)S(1)} %maximum_bitcast_fusion.2), channel_id=1, source_target_pairs={{0,1},{1,2},{2,3},{3,4},{4,5},{5,6},{6,7},{8,9},{9,10},{10,11},{11... | collective-permute-start | bytes 98312 | tf_op jit(solution)/shard_map/ppermute | solution.py:22
  239.7 1.5 collective-permute-done.18
  242.8 4.6 %collective-permute-done.19 = f32[8,8,1,1,128]{4,0,1,3,2:T(8,128)S(1)} collective-permute-done((f32[8,8,1,1,128]{4,0,1,3,2:T(8,128)S(1)}, f32[8,8,1,1,128]{4,0,1,3,2:T(8,128)S(1)}, u32[]{:S(2)}, u32[]{:S(2)}) %collective-permute-start.19) | collective-permute-done | bytes 32800 | tf_op jit(solution)/shard_map/ppermute | solution.py:24
  248.8 42.9 %all-reduce.28 = (f32[]{:T(128)}, f32[]{:T(128)}) all-reduce(f32[]{:T(128)} %get-tuple-element.77, f32[]{:T(128)} %get-tuple-element.76), channel_id=1, replica_groups=mesh['gx'=4,'gy'=8] {'gx','gy'}, use_global_device_ids=true, to_apply=%region_7.14 | all-reduce | flops 2 | bytes 16 | tf_op jit(solution)/shard_map/psum | solution.py:382
  (206 shorter events, 41.7 us)
Async XLA Ops:
  0.6 4.8 %copy-start.5 = (f32[8]{0:T(128)S(1)}, f32[8]{0:T(128)}, u32[]{:S(2)}) copy-start(f32[8]{0:T(128)} %constant.257.clone) | copy-start | bytes 100
  0.6 4.9 %copy-start.6 = (f32[8]{0:T(128)S(1)}, f32[8]{0:T(128)}, u32[]{:S(2)}) copy-start(f32[8]{0:T(128)} %constant.260.clone) | copy-start | bytes 100
  0.7 4.9 %copy-start.7 = (f32[8]{0:T(128)S(1)}, f32[8]{0:T(128)}, u32[]{:S(2)}) copy-start(f32[8]{0:T(128)} %constant.458) | copy-start | bytes 100
  0.7 5.3 %copy-start.3 = (f32[8,8,8,1,1,128]{5,4,3,2,1,0:T(1,128)S(1)}, f32[8,8,8,1,1,128]{5,4,3,2,1,0:T(1,128)}, u32[]{:S(2)}) copy-start(f32[8,8,8,1,1,128]{5,4,3,2,1,0:T(1,128)} %param.19) | copy-start | bytes 786436
  1.5 4.6 %collective-permute-start = (f32[8,8,1,1,128]{4,1,0,3,2:T(8,128)S(1)}, f32[8,8,1,1,128]{4,1,0,3,2:T(8,128)S(1)}, u32[]{:S(2)}, u32[]{:S(2)}) collective-permute-start(f32[8,8,1,1,128]{4,1,0,3,2:T(8,128)S(1)} %get-tuple-element.128), channel_id=1, source_target_pairs={{0,8},{8,16},{16,24},{1,9},{9,17},{17,25},{2,10},{10,18},{18,26},{... | collective-permute-start | bytes 98312 | tf_op jit(solution)/shard_map/ppermute | solution.py:22
  3.9 5.2 %collective-permute-start.1 = (f32[8,8,1,1,128]{4,1,0,3,2:T(8,128)S(1)}, f32[8,8,1,1,128]{4,1,0,3,2:T(8,128)S(1)}, u32[]{:S(2)}, u32[]{:S(2)}) collective-permute-start(f32[8,8,1,1,128]{4,1,0,3,2:T(8,128)S(1)} %get-tuple-element.129), channel_id=1, source_target_pairs={{8,0},{16,8},{24,16},{9,1},{17,9},{25,17},{10,2},{18,10},{26,18},{... | collective-permute-start | bytes 98312 | tf_op jit(solution)/shard_map/ppermute | solution.py:24
  9.1 5.0 %collective-permute-start.2 = (f32[8,8,1,1,128]{4,0,1,3,2:T(8,128)S(1)}, f32[8,8,1,1,128]{4,0,1,3,2:T(8,128)S(1)}, u32[]{:S(2)}, u32[]{:S(2)}) collective-permute-start(f32[8,8,1,1,128]{4,0,1,3,2:T(8,128)S(1)} %maximum_bitcast_fusion.16), channel_id=1, source_target_pairs={{0,1},{1,2},{2,3},{3,4},{4,5},{5,6},{6,7},{8,9},{9,10},{10,11},{11... | collective-permute-start | bytes 98312 | tf_op jit(solution)/shard_map/ppermute | solution.py:22
  14.1 6.1 %collective-permute-start.3 = (f32[8,8,1,1,128]{4,0,1,3,2:T(8,128)S(1)}, f32[8,8,1,1,128]{4,0,1,3,2:T(8,128)S(1)}, u32[]{:S(2)}, u32[]{:S(2)}) collective-permute-start(f32[8,8,1,1,128]{4,0,1,3,2:T(8,128)S(1)} %get-tuple-element.103), channel_id=1, source_target_pairs={{1,0},{2,1},{3,2},{4,3},{5,4},{6,5},{7,6},{9,8},{10,9},{11,10},{12... | collective-permute-start | bytes 98312 | tf_op jit(solution)/shard_map/ppermute | solution.py:24
  20.8 0.7 copy-start.4
  68.3 0.7 copy-start.2
  71.6 3.0 %collective-permute-start.4 = (f32[8,8,1,1,128]{4,1,0,3,2:T(8,128)S(1)}, f32[8,8,1,1,128]{4,1,0,3,2:T(8,128)S(1)}, u32[]{:S(2)}, u32[]{:S(2)}) collective-permute-start(f32[8,8,1,1,128]{4,1,0,3,2:T(8,128)S(1)} %get-tuple-element.124), channel_id=1, source_target_pairs={{0,8},{8,16},{16,24},{1,9},{9,17},{17,25},{2,10},{10,18},{18,26},{... | collective-permute-start | bytes 98312 | tf_op jit(solution)/shard_map/ppermute | solution.py:22
  72.9 5.6 %collective-permute-start.5 = (f32[8,8,1,1,128]{4,1,0,3,2:T(8,128)S(1)}, f32[8,8,1,1,128]{4,1,0,3,2:T(8,128)S(1)}, u32[]{:S(2)}, u32[]{:S(2)}) collective-permute-start(f32[8,8,1,1,128]{4,1,0,3,2:T(8,128)S(1)} %get-tuple-element.125), channel_id=1, source_target_pairs={{8,0},{16,8},{24,16},{9,1},{17,9},{25,17},{10,2},{18,10},{26,18},{... | collective-permute-start | bytes 98312 | tf_op jit(solution)/shard_map/ppermute | solution.py:24
  78.6 4.1 %collective-permute-start.6 = (f32[8,8,1,1,128]{4,1,0,3,2:T(8,128)S(1)}, f32[8,8,1,1,128]{4,1,0,3,2:T(8,128)S(1)}, u32[]{:S(2)}, u32[]{:S(2)}) collective-permute-start(f32[8,8,1,1,128]{4,1,0,3,2:T(8,128)S(1)} %maximum_bitcast_fusion.12), channel_id=1, source_target_pairs={{0,1},{1,2},{2,3},{3,4},{4,5},{5,6},{6,7},{8,9},{9,10},{10,11},{11... | collective-permute-start | bytes 98312 | tf_op jit(solution)/shard_map/ppermute | solution.py:22
  82.7 6.1 %collective-permute-start.7 = (f32[8,8,1,1,128]{4,1,0,3,2:T(8,128)S(1)}, f32[8,8,1,1,128]{4,1,0,3,2:T(8,128)S(1)}, u32[]{:S(2)}, u32[]{:S(2)}) collective-permute-start(f32[8,8,1,1,128]{4,1,0,3,2:T(8,128)S(1)} %get-tuple-element.101), channel_id=1, source_target_pairs={{1,0},{2,1},{3,2},{4,3},{5,4},{6,5},{7,6},{9,8},{10,9},{11,10},{12... | collective-permute-start | bytes 98312 | tf_op jit(solution)/shard_map/ppermute | solution.py:24
  89.1 0.7 copy-start.1
  90.2 1.0 copy-start
  93.6 4.0 %collective-permute-start.8 = (f32[8,8,1,1,128]{4,1,0,3,2:T(8,128)S(1)}, f32[8,8,1,1,128]{4,1,0,3,2:T(8,128)S(1)}, u32[]{:S(2)}, u32[]{:S(2)}) collective-permute-start(f32[8,8,1,1,128]{4,1,0,3,2:T(8,128)S(1)} %get-tuple-element.118), channel_id=1, source_target_pairs={{0,8},{8,16},{16,24},{1,9},{9,17},{17,25},{2,10},{10,18},{18,26},{... | collective-permute-start | bytes 98312 | tf_op jit(solution)/shard_map/ppermute | solution.py:22
  96.1 4.6 %collective-permute-start.9 = (f32[8,8,1,1,128]{4,1,0,3,2:T(8,128)S(1)}, f32[8,8,1,1,128]{4,1,0,3,2:T(8,128)S(1)}, u32[]{:S(2)}, u32[]{:S(2)}) collective-permute-start(f32[8,8,1,1,128]{4,1,0,3,2:T(8,128)S(1)} %get-tuple-element.119), channel_id=1, source_target_pairs={{8,0},{16,8},{24,16},{9,1},{17,9},{25,17},{10,2},{18,10},{26,18},{... | collective-permute-start | bytes 98312 | tf_op jit(solution)/shard_map/ppermute | solution.py:24
  100.8 6.4 %collective-permute-start.10 = (f32[8,8,1,1,128]{4,0,1,3,2:T(8,128)S(1)}, f32[8,8,1,1,128]{4,0,1,3,2:T(8,128)S(1)}, u32[]{:S(2)}, u32[]{:S(2)}) collective-permute-start(f32[8,8,1,1,128]{4,0,1,3,2:T(8,128)S(1)} %maximum_bitcast_fusion.10), channel_id=1, source_target_pairs={{0,1},{1,2},{2,3},{3,4},{4,5},{5,6},{6,7},{8,9},{9,10},{10,11},{11... | collective-permute-start | bytes 98312 | tf_op jit(solution)/shard_map/ppermute | solution.py:22
  107.2 6.1 %collective-permute-start.11 = (f32[8,8,1,1,128]{4,0,1,3,2:T(8,128)S(1)}, f32[8,8,1,1,128]{4,0,1,3,2:T(8,128)S(1)}, u32[]{:S(2)}, u32[]{:S(2)}) collective-permute-start(f32[8,8,1,1,128]{4,0,1,3,2:T(8,128)S(1)} %get-tuple-element.97), channel_id=1, source_target_pairs={{1,0},{2,1},{3,2},{4,3},{5,4},{6,5},{7,6},{9,8},{10,9},{11,10},{12... | collective-permute-start | bytes 98312 | tf_op jit(solution)/shard_map/ppermute | solution.py:24
  206.6 3.3 %collective-permute-start.12 = (f32[8,8,1,1,128]{4,1,0,3,2:T(8,128)S(1)}, f32[8,8,1,1,128]{4,1,0,3,2:T(8,128)S(1)}, u32[]{:S(2)}, u32[]{:S(2)}) collective-permute-start(f32[8,8,1,1,128]{4,1,0,3,2:T(8,128)S(1)} %get-tuple-element.114), channel_id=1, source_target_pairs={{0,8},{8,16},{16,24},{1,9},{9,17},{17,25},{2,10},{10,18},{18,26},{... | collective-permute-start | bytes 98312 | tf_op jit(solution)/shard_map/ppermute | solution.py:22
  207.9 5.6 %collective-permute-start.13 = (f32[8,8,1,1,128]{4,1,0,3,2:T(8,128)S(1)}, f32[8,8,1,1,128]{4,1,0,3,2:T(8,128)S(1)}, u32[]{:S(2)}, u32[]{:S(2)}) collective-permute-start(f32[8,8,1,1,128]{4,1,0,3,2:T(8,128)S(1)} %get-tuple-element.115), channel_id=1, source_target_pairs={{8,0},{16,8},{24,16},{9,1},{17,9},{25,17},{10,2},{18,10},{26,18},{... | collective-permute-start | bytes 98312 | tf_op jit(solution)/shard_map/ppermute | solution.py:24
  213.6 4.1 %collective-permute-start.14 = (f32[8,8,1,1,128]{4,0,1,3,2:T(8,128)S(1)}, f32[8,8,1,1,128]{4,0,1,3,2:T(8,128)S(1)}, u32[]{:S(2)}, u32[]{:S(2)}) collective-permute-start(f32[8,8,1,1,128]{4,0,1,3,2:T(8,128)S(1)} %maximum_bitcast_fusion.6), channel_id=1, source_target_pairs={{0,1},{1,2},{2,3},{3,4},{4,5},{5,6},{6,7},{8,9},{9,10},{10,11},{11... | collective-permute-start | bytes 98312 | tf_op jit(solution)/shard_map/ppermute | solution.py:22
  217.7 6.1 %collective-permute-start.15 = (f32[8,8,1,1,128]{4,0,1,3,2:T(8,128)S(1)}, f32[8,8,1,1,128]{4,0,1,3,2:T(8,128)S(1)}, u32[]{:S(2)}, u32[]{:S(2)}) collective-permute-start(f32[8,8,1,1,128]{4,0,1,3,2:T(8,128)S(1)} %get-tuple-element.93), channel_id=1, source_target_pairs={{1,0},{2,1},{3,2},{4,3},{5,4},{6,5},{7,6},{9,8},{10,9},{11,10},{12... | collective-permute-start | bytes 98312 | tf_op jit(solution)/shard_map/ppermute | solution.py:24
  227.6 4.3 %collective-permute-start.16 = (f32[8,8,1,1,128]{4,1,0,3,2:T(8,128)S(1)}, f32[8,8,1,1,128]{4,1,0,3,2:T(8,128)S(1)}, u32[]{:S(2)}, u32[]{:S(2)}) collective-permute-start(f32[8,8,1,1,128]{4,1,0,3,2:T(8,128)S(1)} %get-tuple-element.110), channel_id=1, source_target_pairs={{0,8},{8,16},{16,24},{1,9},{9,17},{17,25},{2,10},{10,18},{18,26},{... | collective-permute-start | bytes 98312 | tf_op jit(solution)/shard_map/ppermute | solution.py:22
  230.2 4.6 %collective-permute-start.17 = (f32[8,8,1,1,128]{4,1,0,3,2:T(8,128)S(1)}, f32[8,8,1,1,128]{4,1,0,3,2:T(8,128)S(1)}, u32[]{:S(2)}, u32[]{:S(2)}) collective-permute-start(f32[8,8,1,1,128]{4,1,0,3,2:T(8,128)S(1)} %get-tuple-element.111), channel_id=1, source_target_pairs={{8,0},{16,8},{24,16},{9,1},{17,9},{25,17},{10,2},{18,10},{26,18},{... | collective-permute-start | bytes 98312 | tf_op jit(solution)/shard_map/ppermute | solution.py:24
  234.8 6.4 %collective-permute-start.18 = (f32[8,8,1,1,128]{4,0,1,3,2:T(8,128)S(1)}, f32[8,8,1,1,128]{4,0,1,3,2:T(8,128)S(1)}, u32[]{:S(2)}, u32[]{:S(2)}) collective-permute-start(f32[8,8,1,1,128]{4,0,1,3,2:T(8,128)S(1)} %maximum_bitcast_fusion.2), channel_id=1, source_target_pairs={{0,1},{1,2},{2,3},{3,4},{4,5},{5,6},{6,7},{8,9},{9,10},{10,11},{11... | collective-permute-start | bytes 98312 | tf_op jit(solution)/shard_map/ppermute | solution.py:22
  241.3 6.1 %collective-permute-start.19 = (f32[8,8,1,1,128]{4,0,1,3,2:T(8,128)S(1)}, f32[8,8,1,1,128]{4,0,1,3,2:T(8,128)S(1)}, u32[]{:S(2)}, u32[]{:S(2)}) collective-permute-start(f32[8,8,1,1,128]{4,0,1,3,2:T(8,128)S(1)} %get-tuple-element.87), channel_id=1, source_target_pairs={{1,0},{2,1},{3,2},{4,3},{5,4},{6,5},{7,6},{9,8},{10,9},{11,10},{12... | collective-permute-start | bytes 98312 | tf_op jit(solution)/shard_map/ppermute | solution.py:24
where the time goes:
time: 300 us; the launch traced here: 298 us
  blocking collectives  170 us (57%)
  waiting for transfers between devices  45.5 us (15%)
  starting transfers between devices  41.4 us (14%)
  matrix products  19.2 us (6%)
  other arithmetic  7.82 us (3%)
  between operations  7.73 us (3%)
  local copies, waits for them, and re-layouts  6.3 us (2%)
    psum x2, blocking collectives, pair_total(): lax.psum((inner_sum(left, middle_vec), inner_sum(middle_vec, right)), ('g...  85.8 us
    psum x2, blocking collectives, coarse_part(): whole_grid = lax.psum(whole_grid, ('gx', 'gy'))  84.4 us
    ppermute x10, waiting for transfers between devices, with_halo(): lax.ppermute(head, axis, [((i + 1) % count, i) for i in range(ends)])  39.1 us
    ppermute x10, starting transfers between devices, with_halo(): lax.ppermute(tail, axis, [(i, (i + 1) % count) for i in range(ends)])  28.1 us
    dot_general x48, matrix products, contract(): return jnp.einsum(form, table, field, precision=lax.Precision.HIGHEST)  19.2 us
    ppermute x10, starting transfers between devices, with_halo(): lax.ppermute(head, axis, [((i + 1) % count, i) for i in range(ends)])  13.3 us
    ppermute x10, waiting for transfers between devices, with_halo(): lax.ppermute(tail, axis, [(i, (i + 1) % count) for i in range(ends)])  6.37 us
  transfers between devices with their start and end apart: 20, of which 15 were waited for; matrix products, arithmetic and copies ran while one was open for 2% of the time, Pallas kernels for 0%

commit v1 on v0

v1 whole, which is shorter than its diff:
```python
import functools
import math

import jax
import jax.numpy as jnp
import numpy as np
from jax import lax
from jax.experimental import pallas as pl
from jax.experimental.pallas import tpu as pltpu
from jax.sharding import PartitionSpec as P

MESH = pl.DeviceIdType.MESH
stretch = (1.0, 64.0, 1.0)
DIRS = ((-1, 0), (1, 0), (0, -1), (0, 1), (-1, -1), (-1, 1), (1, -1), (1, 1))


def legendre_value(order, position):
    prev_value = 1.0
    this_value = position
    for degree_now in range(2, order + 1):
        next_value = (
            (2 * degree_now - 1) * position * this_value - (degree_now - 1) * prev_value
        ) / degree_now
        prev_value = this_value
        this_value = next_value
    return this_value


def gll_points():
    points = [-1.0]
    for node_index in range(1, 7):
        position = -math.cos(math.pi * node_index / 7.0)
        for newton_step in range(60):
            target = legendre_value(8, position) - legendre_value(6, position)
            slope = 15.0 * legendre_value(7, position)
            position = position - target / slope
        points.append(position)
    points.append(1.0)
    return points


def jacobi_eigen(matrix_in):
    order_n = len(matrix_in)
    work_mat = [list(one_row) for one_row in matrix_in]
    vectors = [
        [1.0 if row_index == col_index else 0.0 for col_index in range(order_n)]
        for row_index in range(order_n)
    ]
    for sweep_index in range(40):
        for first_idx in range(order_n):
            for second_idx in range(first_idx + 1, order_n):
                rotation = 0.5 * math.atan2(
                    2.0 * work_mat[first_idx][second_idx],
                    work_mat[second_idx][second_idx] - work_mat[first_idx][first_idx],
                )
                cosine = math.cos(rotation)
                sine_part = math.sin(rotation)
                for other in range(order_n):
                    left_val = work_mat[other][first_idx]
                    right_val = work_mat[other][second_idx]
                    work_mat[other][first_idx] = cosine * left_val - sine_part * right_val
                    work_mat[other][second_idx] = sine_part * left_val + cosine * right_val
                for other in range(order_n):
                    left_val = work_mat[first_idx][other]
                    right_val = work_mat[second_idx][other]
                    work_mat[first_idx][other] = cosine * left_val - sine_part * right_val
                    work_mat[second_idx][other] = sine_part * left_val + cosine * right_val
                for other in range(order_n):
                    left_val = vectors[other][first_idx]
                    right_val = vectors[other][second_idx]
                    vectors[other][first_idx] = cosine * left_val - sine_part * right_val
                    vectors[other][second_idx] = sine_part * left_val + cosine * right_val
    return ([work_mat[diag_index][diag_index] for diag_index in range(order_n)], vectors)


def spectral_tables():
    nodes = gll_points()
    values_at = [legendre_value(7, position) for position in nodes]
    weights = [2.0 / (56.0 * value_now * value_now) for value_now in values_at]
    derivative = np.zeros((8, 8))
    for row in range(8):
        for col in range(8):
            if row != col:
                derivative[row, col] = values_at[row] / (
                    values_at[col] * (nodes[row] - nodes[col])
                )
    derivative[0, 0] = -14.0
    derivative[7, 7] = 14.0
    weights = np.array(weights)
    stiffness = derivative.T @ np.diag(weights) @ derivative
    stiffness[0, 0] *= 2.0
    stiffness[7, 7] *= 2.0
    inv_root = 1.0 / np.sqrt(weights)
    symmetric = inv_root[:, None] * stiffness * inv_root[None, :]
    eigen_values, eigen_vectors = jacobi_eigen(symmetric.tolist())
    fdm_basis = inv_root[:, None] * np.array(eigen_vectors)
    nodes = np.array(nodes)
    hats = np.stack([(1.0 - nodes) / 2.0, (1.0 + nodes) / 2.0])
    return weights, derivative, fdm_basis, np.array(eigen_values), hats


def sine_table(cells):
    ids = np.arange(cells + 1)
    table = math.sqrt(2.0 / cells) * np.sin(math.pi * (np.outer(ids, ids) % (2 * cells)) / cells)
    table[0] = table[-1] = 0.0
    table[:, 0] = table[:, -1] = 0.0
    return table


def mode_values(cells):
    cosines = np.cos(math.pi * np.arange(1, cells) / cells)
    return (2.0 - 2.0 * cosines) / 2.0, 2.0 * (4.0 + 2.0 * cosines) / 6.0


def round_up(value, step):
    return -(-value // step) * step


def halves(table):
    table = np.asarray(table, np.float32)
    high = table.astype(jnp.bfloat16)
    low = (table - high.astype(np.float32)).astype(jnp.bfloat16)
    return np.concatenate([high, low], axis=0)


def element_tables():
    weights, derivative, basis, eigen, hats = spectral_tables()
    eye = np.eye(8)
    cube = np.kron(np.kron(basis, basis), basis)
    total = (
        stretch[0] * eigen[:, None, None]
        + stretch[1] * eigen[None, :, None]
        + stretch[2] * eigen[None, None, :]
    ).reshape(-1)
    solve = (cube / total) @ cube.T
    along_j = np.kron(np.eye(4), np.kron(derivative, eye))
    along_k = np.kron(np.eye(4), np.kron(eye, derivative))
    forward = np.concatenate([along_j, along_k], axis=0)
    backward = np.concatenate([stretch[1] * along_j.T, stretch[2] * along_k.T], axis=1)
    corner = np.stack(
        [
            np.kron(np.kron(hats[a], hats[b]), hats[c])
            for c in range(2)
            for a in range(2)
            for b in range(2)
        ]
    )
    return weights, derivative, solve, forward, backward, corner


def coarse_tables(size_x, size_y, depth):
    sine_x, sine_y, sine_z = sine_table(size_x), sine_table(size_y), sine_table(depth)
    modes = (size_x - 1) * (size_y - 1)
    rows = round_up(modes + 2, 8)
    gather = np.zeros((rows, size_x, size_y, 4))
    for x in range(size_x):
        for y in range(size_y):
            for a in range(2):
                for b in range(2):
                    gather[:modes, x, y, 2 * a + b] = np.outer(
                        sine_x[1:-1, x + a], sine_y[1:-1, y + b]
                    ).reshape(-1)
    for q in range(2):
        gather[modes + q, :, :, q] = 1.0
    stiff_x, mass_x = mode_values(size_x)
    stiff_y, mass_y = mode_values(size_y)
    stiff_z, mass_z = mode_values(depth)
    denominator = (
        stretch[0] * stiff_x[:, None, None] * mass_y[None, :, None] * mass_z[None, None, :]
        + stretch[1] * mass_x[:, None, None] * stiff_y[None, :, None] * mass_z[None, None, :]
        + stretch[2] * mass_x[:, None, None] * mass_y[None, :, None] * stiff_z[None, None, :]
    )
    inverse = np.zeros((rows, depth))
    inverse[:modes, 1:] = (1.0 / denominator).reshape(modes, depth - 1)
    back = np.zeros((size_x, size_y, 8, rows))
    for x in range(size_x):
        for y in range(size_y):
            for c in range(2):
                for a in range(2):
                    for b in range(2):
                        back[x, y, 4 * c + 2 * a + b, :modes] = np.outer(
                            sine_x[1:-1, x + a], sine_y[1:-1, y + b]
                        ).reshape(-1)
    return (
        gather.reshape(rows, -1),
        inverse,
        back.reshape(size_x * size_y, 8, rows),
        sine_z[:depth, :depth],
    )


def parts(field):
    high = field.astype(jnp.bfloat16)
    return high, (field - high.astype(jnp.float32)).astype(jnp.bfloat16)


def both_dot(left, right):
    rows, lanes = left.shape[0], right.shape[1]
    sums = jnp.dot(
        jnp.concatenate(parts(left), axis=0),
        jnp.concatenate(parts(right), axis=1),
        preferred_element_type=jnp.float32,
    )
    return (sums[:rows, :lanes] + sums[rows:, :lanes]) + (sums[:rows, lanes:] + sums[rows:, lanes:])


def split_dot(table, field):
    lanes = field.shape[1]
    rows = table.shape[0] // 2
    high = field.astype(jnp.bfloat16)
    low = (field - high.astype(jnp.float32)).astype(jnp.bfloat16)
    both = jnp.concatenate([high, low], axis=1)
    top = jnp.dot(table[:rows], both, preferred_element_type=jnp.float32)
    bottom = jnp.dot(table[rows:], both, preferred_element_type=jnp.float32)
    return (top[:, :lanes] + bottom[:, :lanes]) + (top[:, lanes:] + bottom[:, lanes:])


def kernel(size_x, size_y, weights, derivative, modes, *refs):
    n_in = 11
    inputs, (p_ref, r_ref) = refs[:n_in], refs[n_in : n_in + 2]
    local = refs[n_in + 2 : 2 * n_in + 2]
    (
        cw, out, base, first, second, image, alpha, beta_raw, smooth,
        rx, ry, re, message_ref, got,
        in_sem, halo_send, halo_recv, all_send, all_recv,
    ) = refs[2 * n_in + 2 :]
    (
        f_ref, corner_ref, coef_ref, weight_ref, solve_ref,
        gather_ref, sine_ref, inverse_ref, back_ref, forward_ref, backward_ref,
    ) = local
    lanes = f_ref.shape[2]
    my_x = lax.axis_index("gx")
    my_y = lax.axis_index("gy")
    devices = size_x * size_y
    me = my_x * size_y + my_y

    fetches = [
        pltpu.make_async_copy(inputs[n], local[n], in_sem.at[n]) for n in range(n_in)
    ]
    for fetch in fetches:
        fetch.start()

    def exists(direction):
        dx, dy = direction
        ok = None
        for pos, size, step in ((my_x, size_x, dx), (my_y, size_y, dy)):
            if step:
                cond = pos > 0 if step < 0 else pos < size - 1
                ok = cond if ok is None else jnp.logical_and(ok, cond)
        return ok

    def peer(offset):
        other = lax.rem(me + offset, devices)
        return (other // size_y, lax.rem(other, size_y))

    barrier = pltpu.get_barrier_semaphore()

    @pl.loop(1, devices)
    def _(offset):
        pl.semaphore_signal(barrier, inc=1, device_id=peer(offset), device_id_type=MESH)

    def node_rows(step):
        return 0 if step < 0 else 7

    def source(direction):
        dx, dy = direction
        if dy == 0:
            return out.at[node_rows(dx)]
        ys = pl.ds(8 * node_rows(dy), 8)
        if dx == 0:
            return out.at[:, ys]
        return out.at[node_rows(dx), ys]

    def landing(turn, index):
        if index < 2:
            return rx.at[turn, index]
        if index < 4:
            return ry.at[turn, index - 2]
        return re.at[turn, index - 4]

    def halo_copy(turn, index):
        direction = DIRS[index]
        opposite = DIRS.index((-direction[0], -direction[1]))
        return pltpu.make_async_remote_copy(
            src_ref=source(direction),
            dst_ref=landing(turn, opposite),
            send_sem=halo_send.at[turn, index],
            recv_sem=halo_recv.at[turn, opposite],
            device_id=(my_x + direction[0], my_y + direction[1]),
            device_id_type=MESH,
        )

    def halo_arrival(turn, index):
        direction = DIRS[index]
        return pltpu.make_async_remote_copy(
            src_ref=source(direction),
            dst_ref=landing(turn, index),
            send_sem=halo_send.at[turn, index],
            recv_sem=halo_recv.at[turn, index],
            device_id=(my_x + direction[0], my_y + direction[1]),
            device_id_type=MESH,
        )

    lane = lax.broadcasted_iota(jnp.int32, (8, 8, lanes), 2)

    def sum_depth(raw):
        out[...] = raw
        head = out[:, pl.ds(0, 8, stride=8), :]
        tail = out[:, pl.ds(7, 8, stride=8), :]
        from_tail = pltpu.roll(tail.reshape(64, lanes), 1, 1).reshape(8, 8, lanes)
        from_head = pltpu.roll(head.reshape(64, lanes), lanes - 1, 1).reshape(8, 8, lanes)
        out[:, pl.ds(0, 8, stride=8), :] = jnp.where(lane == 0, 0.0, head + from_tail)
        out[:, pl.ds(7, 8, stride=8), :] = jnp.where(lane == lanes - 1, 0.0, tail + from_head)

    def send_halo(turn):
        for index in range(8):
            @pl.when(exists(DIRS[index]))
            def _(index=index):
                halo_copy(turn, index).start()

    def take_halo(turn, target):
        for index in range(8):
            @pl.when(exists(DIRS[index]))
            def _(index=index):
                halo_copy(turn, index).wait_send()
                halo_arrival(turn, index).wait_recv()

        has = [exists(direction) for direction in DIRS[:4]]
        target[pl.ds(1, 6), pl.ds(8, 48)] = out[pl.ds(1, 6), pl.ds(8, 48)]
        for side in range(2):
            i = 7 * side
            target[i, pl.ds(8, 48)] = jnp.where(
                has[side], out[i, pl.ds(8, 48)] + rx[turn, side, pl.ds(8, 48)], 0.0
            )
            target[pl.ds(1, 6), pl.ds(8 * i, 8)] = jnp.where(
                has[2 + side],
                out[pl.ds(1, 6), pl.ds(8 * i, 8)] + ry[turn, side, pl.ds(1, 6)],
                0.0,
            )
            for other in range(2):
                j = 7 * other
                target[i, pl.ds(8 * j, 8)] = jnp.where(
                    jnp.logical_and(has[side], has[2 + other]),
                    (out[i, pl.ds(8 * j, 8)] + rx[turn, side, pl.ds(8 * j, 8)])
                    + (ry[turn, other, i] + re[turn, 2 * side + other]),
                    0.0,
                )

    def send_all(turn, value):
        message_ref[turn] = value
        got[turn, me] = value

        @pl.loop(1, devices)
        def _(offset):
            pltpu.make_async_remote_copy(
                src_ref=message_ref.at[turn],
                dst_ref=got.at[turn, me],
                send_sem=all_send.at[turn],
                recv_sem=all_recv.at[turn],
                device_id=peer(offset),
                device_id_type=MESH,
            ).start()

    def take_all(turn):
        span = got.at[turn, pl.ds(0, devices - 1)]
        copy = pltpu.make_async_remote_copy(
            src_ref=span,
            dst_ref=span,
            send_sem=all_send.at[turn],
            recv_sem=all_recv.at[turn],
            device_id=peer(1),
            device_id_type=MESH,
        )
        copy.wait_send()
        copy.wait_recv()
        return got[turn]

    row = lax.broadcasted_iota(jnp.int32, (8, lanes), 0)
    row4 = lax.broadcasted_iota(jnp.int32, (4, lanes), 0)
    lane4 = lax.broadcasted_iota(jnp.int32, (4, lanes), 1)

    def corner_message(raw):
        corners = both_dot(corner_ref[...], raw)
        moved = pltpu.roll(pltpu.roll(corners, 1, 1), 4, 0)
        return (corners + moved)[:4]

    def coarse_values(turn):
        gathered = take_all(turn).reshape(devices * 4, lanes)
        combined = both_dot(gather_ref[...], gathered)
        spectral = both_dot(combined, sine_ref[...]) * inverse_ref[...]
        mine = both_dot(back_ref[me], spectral)
        columns = both_dot(mine, sine_ref[...])
        corners = jnp.where(row < 4, columns, pltpu.roll(columns, lanes - 1, 1))
        return both_dot(corner_ref[...].T, corners), combined

    def local_solve(field):
        return split_dot(solve_ref[...], field).reshape(8, 64, lanes)

    def stiffness(field_ref, target):
        for half in range(2):
            span = pl.ds(4 * half, 4)
            values = field_ref[span] - field_ref[span, pl.ds(27, 1)]
            grads = split_dot(forward_ref[...], values.reshape(256, lanes))
            factor = cw[span].reshape(256, lanes)
            flux = jnp.concatenate([grads[:256] * factor, grads[256:] * factor], axis=0)
            target[span] = split_dot(backward_ref[...], flux).reshape(4, 64, lanes)
        for part in range(8):
            span = pl.ds(8 * part, 8)
            values = [field_ref[i, span] for i in range(8)]
            flux = []
            for p in range(8):
                grad = values[0] * derivative[p][0]
                for i in range(1, 8):
                    grad = grad + values[i] * derivative[p][i]
                flux.append(grad * cw[p, span])
            for i in range(8):
                total = target[i, span]
                for p in range(8):
                    total = total + flux[p] * derivative[p][i]
                target[i, span] = total

    def partial(left, right):
        return jnp.sum((left * right).reshape(64, 8, lanes), axis=0)

    def row_sum(tile):
        return jnp.sum(tile, axis=0, keepdims=True)

    def total(rows):
        return jnp.sum(rows, axis=(0, 1), keepdims=True)

    fetches[0].wait()
    sum_depth(f_ref[...])
    pl.semaphore_wait(barrier, devices - 1)
    send_halo(0)
    fetches[1].wait()
    send_all(0, corner_message(f_ref[...].reshape(512, lanes)))
    fetches[2].wait()
    fetches[3].wait()
    for i in range(8):
        cw[i] = coef_ref[i] * (weight_ref[...] * weights[i])
    for fetch in fetches[4:]:
        fetch.wait()
    take_halo(0, base)

    sum_depth(local_solve(base[...].reshape(512, lanes)))
    send_halo(1)
    coarse, _ = coarse_values(0)
    take_halo(1, first)
    first[...] += coarse.reshape(8, 64, lanes)

    stiffness(first, alpha)
    sum_depth(alpha[...])
    send_halo(2)
    message = corner_message(alpha[...].reshape(512, lanes))
    energy = total(partial(f_ref[...], first[...]))
    curve = total(partial(alpha[...], first[...]))
    message = jnp.where(
        lane4 == 0, jnp.where(row4 == 0, energy, jnp.where(row4 == 1, curve, 0.0)), message
    )
    send_all(1, message)
    take_halo(2, image)

    sum_depth(local_solve(image[...].reshape(512, lanes)))
    send_halo(3)
    coarse, combined = coarse_values(1)
    energy = combined[modes : modes + 1, 0:1]
    curve = combined[modes + 1 : modes + 2, 0:1]
    step = energy / curve
    take_halo(3, smooth)
    step3 = step.reshape(1, 1, 1)
    second[...] = first[...] - step3 * (smooth[...] + coarse.reshape(8, 64, lanes))

    stiffness(second, beta_raw)
    sum_depth(beta_raw[...])
    send_halo(4)
    fresh = row_sum(partial(f_ref[...] - step3 * alpha[...], second[...]))
    along = row_sum(partial(beta_raw[...], second[...]))
    cross = row_sum(partial(alpha[...], second[...]))
    send_all(
        2,
        jnp.where(
            row4 == 0, fresh, jnp.where(row4 == 1, along, jnp.where(row4 == 2, cross, 0.0))
        ),
    )
    take_halo(4, smooth)
    sums = jnp.sum(take_all(2), axis=0)
    fresh = total(sums[0:1])
    ratio = fresh / energy
    along = total(sums[1:2]) + 2.0 * ratio * total(sums[2:3]) + ratio * ratio * curve
    second_step = fresh / along
    ratio3 = ratio.reshape(1, 1, 1)
    second3 = second_step.reshape(1, 1, 1)
    p_ref[...] = step3 * first[...] + second3 * (second[...] + ratio3 * first[...])
    r_ref[...] = (base[...] - step3 * image[...]) - second3 * (smooth[...] + ratio3 * image[...])


def solution(mesh):
    size_x, size_y = mesh.shape["gx"], mesh.shape["gy"]
    devices = size_x * size_y
    weights, derivative, solve, forward, backward, corner = element_tables()
    spec = P(None, None, None, "gx", "gy", None)

    def on_device(forcing, coefficient):
        shape = forcing.shape
        depth = shape[5]
        gather, inverse, back, sine = coarse_tables(size_x, size_y, depth)
        modes = (size_x - 1) * (size_y - 1)
        plane = np.outer(weights, weights).reshape(64, 1) * np.ones((1, depth))
        single = [
            np.asarray(table, np.float32)
            for table in (corner, plane, gather, sine, inverse, back)
        ]
        field = (8, 64, depth)
        operands = [
            forcing.reshape(field), single[0], coefficient.reshape(field), single[1],
            halves(solve), *single[2:], halves(forward), halves(backward),
        ]
        vmem = pl.BlockSpec(memory_space=pltpu.VMEM)
        pressure, residual = pl.pallas_call(
            functools.partial(
                kernel, size_x, size_y, weights.tolist(), derivative.tolist(), modes
            ),
            out_shape=[jax.ShapeDtypeStruct(field, jnp.float32)] * 2,
            in_specs=[pl.BlockSpec(memory_space=pltpu.HBM)] * len(operands),
            out_specs=[vmem, vmem],
            scratch_shapes=[pltpu.VMEM(op.shape, op.dtype) for op in operands]
            + [pltpu.VMEM(field, jnp.float32)] * 9
            + [
                pltpu.VMEM((5, 2, 64, depth), jnp.float32),
                pltpu.VMEM((5, 2, 8, 8, depth), jnp.float32),
                pltpu.VMEM((5, 4, 8, depth), jnp.float32),
                pltpu.VMEM((3, 4, depth), jnp.float32),
                pltpu.VMEM((3, devices, 4, depth), jnp.float32),
                pltpu.SemaphoreType.DMA((len(operands),)),
                pltpu.SemaphoreType.DMA((5, 8)),
                pltpu.SemaphoreType.DMA((5, 8)),
                pltpu.SemaphoreType.DMA((3,)),
                pltpu.SemaphoreType.DMA((3,)),
            ],
            compiler_params=pltpu.CompilerParams(
                collective_id=0, has_side_effects=True, vmem_limit_bytes=60 * 1024 * 1024
            ),
        )(*operands)
        return pressure.reshape(shape), residual.reshape(shape)

    return jax.shard_map(
        on_device, mesh=mesh, in_specs=(spec, spec), out_specs=(spec, spec), check_vma=False
    )
```

time: 300 us -> 36.4 us (0.12)
  blocking collectives: 170 us -> 0 us
  waiting for transfers between devices: 45.5 us -> 0 us
  starting transfers between devices: 41.4 us -> 0 us
  Pallas kernels: 0 us -> 33.2 us
  matrix products: 19.2 us -> 0 us
  other arithmetic: 7.82 us -> 0 us
  between operations: 7.73 us -> 0.65 us
  local copies, waits for them, and re-layouts: 6.3 us -> 2.42 us
    psum x4 -> x0, blocking collectives: 170 us -> none  [the longest x2 85.8 us: pair_total(): lax.psum((inner_sum(left, middle_vec), inner_sum(middle_vec, right)), ('g...]
    ppermute x20 -> x0, waiting for transfers between devices: 45.5 us -> none  [the longest x10 39.1 us: with_halo(): lax.ppermute(head, axis, [((i + 1) % count, i) for i in range(ends)])]
    ppermute x20 -> x0, starting transfers between devices: 41.4 us -> none  [the longest x10 28.1 us: with_halo(): lax.ppermute(tail, axis, [(i, (i + 1) % count) for i in range(ends)])]
    pallas_call x0 -> x1, Pallas kernels: none -> 33.2 us  [on_device(): pl.pallas_call(functools.partial(kernel, size_x, size_y, weights.tolist()...]
    dot_general x48 -> x0, matrix products: 19.2 us -> none  [contract(): return jnp.einsum(form, table, field, precision=lax.Precision.HIGHEST)]
  transfers between devices with their start and end apart: 20 -> 0, of which waited for: 15 -> 0; matrix products, arithmetic and copies ran while one was open for 2% -> 0% of each run, Pallas kernels for 0% -> 0%
where the time goes in v1:
time: 36.4 us; the launch traced here: 36.3 us
  Pallas kernels  33.2 us (91%)
  local copies, waits for them, and re-layouts  2.42 us (7%)
  between operations  0.65 us (2%)
    pallas_call x1, Pallas kernels, on_device(): pl.pallas_call(functools.partial(kernel, size_x, size_y, weights.tolist()...  33.2 us
    unnamed x4, local copies, waits for them, and re-layouts  2.42 us

profile of v1, /device:TPU:0, one launch (start us, length us, event | category | flops | bytes accessed | tf_op | source)
XLA Modules:
  0.0 36.3 jit_solution(11926368132621452780)
XLA Ops:
  0.6 33.2 %shard_map.122 = (f32[8,64,128]{2,1,0:T(8,128)}, f32[8,64,128]{2,1,0:T(8,128)}) custom-call(f32[8,64,128]{2,1,0:T(8,128)} %bitcast.10, f32[8,512]{1,0:T(8,128)} %constant.18.clone.refs_1_, f32[8,64,128]{2,1,0:T(8,128)} %bitcast.11, f32[64,128]{1,0:T(8,128)} %constant.19.clone.refs_3_, bf16[1024,512]{1,0:T(8,128)(2,1)} %constant.20.clone.refs_4_, ...), custom_call_target="tpu_custom_call" | custom-call | tf_op jit(solution)/shard_map/pallas_call | solution.py:519
  33.8 0.0 copy-start
  33.8 1.7 %copy.17 = f32[8,8,8,1,1,128]{5,4,3,2,1,0:T(1,128)} copy(f32[8,8,8,1,1,128]{5,4,3,2,1,0:T(1,128)} %bitcast.9) | data formatting | bytes 524288
  35.6 0.0 copy-done
  35.6 0.7 %copy.18 = f32[8,8,8,1,1,128]{5,4,3,2,1,0:T(1,128)} copy(f32[8,8,8,1,1,128]{5,4,3,2,1,0:T(1,128)S(1)} %bitcast.8) | data formatting | bytes 524288
Async XLA Ops:
  33.8 1.7 %copy-start = (f32[8,64,128]{2,1,0:T(8,128)S(1)}, f32[8,64,128]{2,1,0:T(8,128)}, u32[]{:S(2)}) copy-start(f32[8,64,128]{2,1,0:T(8,128)} %get-tuple-element.5) | copy-start | bytes 786436
